TPU v7x, 256 devices: a whole 4x4x8 slice. The times are simulated.
256 devices in a mesh: ka: 128 (over z, y, x), ga: 2 (over core).
Axes of the slice: x: 4, y: 4, z: 8, core: 2. Of those that a mesh axis runs over, the one named last changes fastest.
Arguments:
- pair_dens: bfloat16 [4096, 40, 1792], P('ka', None, 'ga'), may hold values from -6 to 6
- counts: int32 [4096], P('ka'), may hold values from 2 to 40, as said below
- q_index: int32 [4096, 2], P('ka'), may hold values from 0 to 1, each once within a row
- w_tiles: bfloat16 [2, 1792, 1792], P(None, 'ga', 'ka'), as said below
- partner: bfloat16 [4096, 2, 40, 1792], P('ka', None, None, 'ga'), may hold values from -0.125 to 0.125
Outputs:
- kernel: float32 [4096, 2, 1600], P('ka')
Inputs may be any that keep to these rules, and one draw needn't show every extreme that they name: `counts`: some k point has 40 pairs; the pairs of the 32 k points of one index of ka sum to at most 960, and some index reaches it; the pairs of indices i and i + 64 together sum to at most 1280, and some such two reach it. Each tile is symmetric: w_tiles[b, g, h] = w_tiles[b, h, g].
All inputs are finite; a program needn't handle non-finite values.
Results may differ from a plain program's by a relative error of at most 0.0029.
Values may be sent and summed in bfloat16 or wider, within the bound.
A program may use at most 128 MiB of HBM per device.

v0:
```python
import jax
import jax.numpy as jnp
from jax import lax
from jax.sharding import PartitionSpec as P


def local(pair_dens, counts, q_index, w_tiles, partner):
    kpoints, pair_slots, half_width = pair_dens.shape
    tile_count = w_tiles.shape[0]
    column_pairs = partner.shape[2]
    flat_rows = pair_dens.reshape(kpoints * pair_slots, half_width)
    partial_all = jnp.einsum(
        "rh,bhc->brc",
        flat_rows,
        lax.all_gather(w_tiles, "ka", axis=2, tiled=True),
        preferred_element_type=jnp.float32,
    )
    screened = lax.psum_scatter(partial_all, "ga", scatter_dimension=2, tiled=True).astype(
        jnp.bfloat16
    )
    tile_grid = screened.reshape(tile_count, kpoints, pair_slots, half_width)
    per_tile = jnp.einsum(
        "bkpg,kjcg->bkjpc", tile_grid, partner, preferred_element_type=jnp.float32
    )
    selector = q_index[None, :, :] == jnp.arange(tile_count, dtype=jnp.int32)[:, None, None]
    chosen = jnp.sum(jnp.where(selector[:, :, :, None, None], per_tile, jnp.float32(0.0)), axis=0)
    summed = lax.psum(chosen, "ga")
    live_mask = (
        jnp.arange(pair_slots, dtype=jnp.int32)[None, None, :, None] < counts[:, None, None, None]
    )
    return jnp.where(live_mask, summed, jnp.float32(0.0)).reshape(
        kpoints, tile_count, pair_slots * column_pairs
    )


def solution(mesh):
    in_specs = (
        P("ka", None, "ga"),
        P("ka"),
        P("ka", None),
        P(None, "ga", "ka"),
        P("ka", None, None, "ga"),
    )
    out_specs = P("ka", None, None)
    return jax.shard_map(local, mesh=mesh, in_specs=in_specs, out_specs=out_specs, check_vma=False)
```

profile of v0, /device:TPU:1, one launch (start us, length us, event | category | flops | bytes accessed | tf_op | source)
XLA Modules:
  0.0 248.7 jit_solution(14408642830650272753)
XLA Ops:
  6.5 0.0 copy-start
  6.5 0.0 all-gather.2.cloned.1.call-start
  6.5 0.7 all-gather.2.cloned.1.call-update
  7.3 0.0 reduce-scatter.2.cloned.1.call-start
  7.3 124.8 %all-gather.2.cloned.1.call-done = bf16[2,896,1792]{1,0,2:T(2,128)(2,1)} async-done(((bf16[2,896,14]{1,0,2:T(2,128)(2,1)}), bf16[2,896,1792]{1,0,2:T(2,128)(2,1)}) %all-gather.2.cloned.1.call-update) | async-done | bytes 6422544 | tf_op jit(solution)/shard_map/all_gather | solution.py:15
  132.1 0.0 copy-done
  132.1 16.3 %convolution_bitcast_fusion = f32[2,1280,1792]{1,2,0:T(8,128)} fusion(bf16[1280,896,1]{1,0,2:T(8,128)(2,1)S(1)} %bitcast.22, bf16[2,896,1792]{1,0,2:T(2,128)(2,1)} %all-gather.2.cloned.1.call-done), kind=kOutput, calls=%fused_computation | convolution fusion | flops 8220835840 | bytes 27066368 | tf_op jit(solution)/shard_map/rh,bhc->brc/dot_general | solution.py:12
  148.4 0.0 copy-start.1
  148.4 0.0 reduce-scatter.2.cloned.1.call-update
  148.4 0.0 all-reduce.2.cloned.1.call-start
  148.5 0.6 copy-done.1
  149.1 0.1 copy.13
  149.2 33.0 %reduce-scatter.2.cloned.1.call-done = f32[2,1280,896]{1,2,0:T(8,128)} async-done(((f32[2,1280,1792]{1,2,0:T(8,128)}), f32[2,1280,896]{1,2,0:T(8,128)}) %reduce-scatter.2.cloned.1.call-update) | async-done | bytes 9175056 | tf_op jit(solution)/shard_map/reduce_scatter | solution.py:18
  182.1 6.1 %convert_element_type.3 = bf16[2,1280,896]{1,2,0:T(8,128)(2,1)} convert(f32[2,1280,896]{1,2,0:T(8,128)} %reduce-scatter.2.cloned.1.call-done) | non-fusion elementwise | flops 2293760 | bytes 13762560 | tf_op jit(solution)/shard_map/convert_element_type | solution.py:18
  188.3 7.3 %copy.15 = bf16[2,1280,896]{2,1,0:T(8,128)(2,1)} copy(bf16[2,1280,896]{1,2,0:T(8,128)(2,1)} %convert_element_type.3) | data formatting | bytes 9175040 | tf_op jit(solution)/shard_map/convert_element_type | solution.py:18
  195.6 0.0 copy-start.2
  195.6 8.5 %fusion.4 = f32[32,2,40,40]{3,2,1,0:T(8,128)} fusion(bf16[32,2,40,896]{3,2,1,0:T(8,128)(2,1)} %param.9, bf16[2,32,40,896,1]{3,2,1,0,4:T(8,128)(2,1)} %bitcast.23, pred[2,32,2]{2,0,1:T(4,128)(4,1)S(1)} %iota_compare_fusion), kind=kOutput, calls=%fused_computation.6 | convolution fusion | flops 367308800 | bytes 9584768 | tf_op jit(solution)/shard_map/bkpg,kjcg->bkjpc/dot_general | solution.py:22
  204.1 0.0 all-reduce.2.cloned.1.call-update
  204.1 0.0 copy-done.2
  204.1 0.1 iota_compare_fusion.1
  204.2 32.5 %all-reduce.2.cloned.1.call-done = f32[32,2,40,40]{3,2,1,0:T(8,128)} async-done(((f32[32,2,40,40]{3,2,1,0:T(8,128)}), f32[32,2,40,40]{3,2,1,0:T(8,128)}) %all-reduce.2.cloned.1.call-update) | async-done | bytes 409616 | tf_op jit(solution)/shard_map/psum | solution.py:27
  236.7 2.6 %broadcast_select_fusion = f32[32,2,40,40]{3,2,1,0:T(8,128)} fusion(f32[32,2,40,40]{3,2,1,0:T(8,128)} %all-reduce.2.cloned.1.call-done, pred[32,40]{1,0:T(8,128)(4,1)S(1)} %iota_compare_fusion.1), kind=kLoop, calls=%fused_computation.7 | loop fusion | flops 102400 | bytes 820480 | tf_op jit(solution)/shard_map/jit(_where)/select_n | solution.py:31
  239.3 2.9 %reshape.39 = f32[32,2,1600]{2,1,0:T(2,128)} reshape(f32[32,2,40,40]{3,2,1,0:T(8,128)} %broadcast_select_fusion) | data formatting | bytes 819200 | tf_op jit(solution)/shard_map/reshape | solution.py:31
  (1 shorter events, 0.0 us)
Async XLA Ops:
  6.5 125.5 %copy-start = (bf16[32,40,896]{2,1,0:T(8,128)(2,1)S(1)}, bf16[32,40,896]{2,1,0:T(8,128)(2,1)}, u32[]{:S(2)}) copy-start(bf16[32,40,896]{2,1,0:T(8,128)(2,1)} %param.5) | copy-start | bytes 6881284
  6.5 125.5 %all-gather.2.cloned.1.call-start = ((), (), s32[]{:S(2)}) async-start(), calls=%async_computation.1 | async-start | bytes 6472704 | tf_op jit(solution)/shard_map/all_gather | solution.py:15
  7.3 174.9 %reduce-scatter.2.cloned.1.call-start = ((), (), s32[]{:S(2)}) async-start(), calls=%async_computation.2 | async-start | bytes 27525120 | tf_op jit(solution)/shard_map/reduce_scatter | solution.py:18
  148.4 0.7 copy-start.1
  148.4 88.3 %all-reduce.2.cloned.1.call-start = ((), (), s32[]{:S(2)}) async-start(), calls=%async_computation.3 | async-start | bytes 2621440 | tf_op jit(solution)/shard_map/psum | solution.py:27
  195.6 8.5 %copy-start.2 = (s32[32]{0:T(128)S(1)}, s32[32]{0:T(128)}, u32[]{:S(2)}) copy-start(s32[32]{0:T(128)} %param.6) | copy-start | bytes 388
Sparse Core Ops, SparseCore 0:
  11.1 120.8 all-gather.1
  148.5 33.5 reduce-scatter.1
  204.2 32.3 all-reduce.1
where the time goes:
time: 249 us
  waiting for transfers between devices  191 us (77%)
  matrix products  24.8 us (10%)
  between operations  13.1 us (5%)
  local copies, waits for them, and re-layouts  10.9 us (4%)
  other arithmetic  8.86 us (4%)
    all_gather x1, waiting for transfers between devices, local(): lax.all_gather(w_tiles, 'ka', axis=2, tiled=True)  125 us
    reduce_scatter x1, waiting for transfers between devices, local(): lax.psum_scatter(partial_all, 'ga', scatter_dimension=2, tiled=True)  33 us
    psum x1, waiting for transfers between devices, local(): summed = lax.psum(chosen, 'ga')  32.5 us
    dot_general x1, matrix products, local(): jnp.einsum('rh,bhc->brc', flat_rows, lax.all_gather(w_tiles, 'ka', axis=2...  16.3 us
    dot_general x1, matrix products, local(): jnp.einsum('bkpg,kjcg->bkjpc', tile_grid, partner, preferred_element_type...  8.51 us
    convert_element_type x1, local copies, waits for them, and re-layouts, local(): lax.psum_scatter(partial_all, 'ga', scatter_dimension=2, tiled=True)  7.29 us
    convert_element_type x1, other arithmetic, local(): lax.psum_scatter(partial_all, 'ga', scatter_dimension=2, tiled=True)  6.14 us
  transfers between devices with their start and end apart: 3, of which 3 were waited for; matrix products, arithmetic and copies ran while one was open for 0% of the time, Pallas kernels for 0%

commit v1 on v0

v1 whole, which is shorter than its diff:
```python
import jax
import jax.numpy as jnp
from jax import lax
from jax.experimental import pallas as pl
from jax.experimental.pallas import tpu as pltpu
from jax.sharding import PartitionSpec as P

MESH = pl.DeviceIdType.MESH
BF16, F32 = jnp.bfloat16, jnp.float32

NX, NY, NZ = 4, 4, 8
NODES = NX * NY * NZ
KP, SLOTS, PC = 32, 40, 40
ROWS = KP * SLOTS
NG, HALF = 1792, 896
BLK, MXU = 128, 256
OWN_ROWS = NG // NODES
TILE = 16
STRIPS = NG // TILE
ANTI = STRIPS // 2
SHIFT = 2 * NX * NY
ZSHIFT = SHIFT // (NX * NY)
MC = 256


def nt(a, b):
    return lax.dot_general(a, b, (((1,), (1,)), ((), ())), preferred_element_type=F32)


def nn(a, b):
    return jnp.dot(a, b, preferred_element_type=F32)


def kernel(pd, part, wt, cnt, qv, qs, out,
           pfull, qfull, praw, qsend, m1, m2, acc, rbuf, wraw, wplace, dbl, wn, kp, mine, other,
           s_loc, s_p0, r_p0, s_d2d, r_d2d, s_1, r_1, s_a2, r_a2, s_z, r_z, s_xy, r_xy):
    ka = lax.axis_index("ka")
    ga = lax.axis_index("ga")
    x, y, z = ka % NX, (ka // NX) % NY, ka // (NX * NY)

    def dev(dz=0, dy=0, dx=0):
        return (((z + dz + NZ) % NZ) * (NX * NY) + ((y + dy + NY) % NY) * NX + (x + dx + NX) % NX, ga)

    sibling = (ka, 1 - ga)
    strip = (ka + NODES - SHIFT) % NODES
    is_strip = strip < STRIPS
    is_anti = jnp.logical_and(strip >= STRIPS, strip < STRIPS + 8)

    bar = pltpu.get_barrier_semaphore()

    def greet(device):
        pl.semaphore_signal(bar, inc=1, device_id=device, device_id_type=MESH)

    t0 = (OWN_ROWS * ka) // TILE
    off = (OWN_ROWS * ka) % TILE
    crosses = off + OWN_ROWS > TILE
    n_waits = jnp.int32(9)
    for d in (1, 2, 3):
        greet(dev(dx=d))
        greet(dev(dy=d))
    greet(dev(dz=1))
    greet(dev(dz=-1))
    greet(sibling)

    first_src = (TILE * strip) // OWN_ROWS

    @pl.when(is_strip)
    def _():
        for a in range(2):
            for c in range(2):
                greet((first_src + a, c))

    @pl.when(is_anti)
    def _():
        for i in range(7):
            src = (TILE * (8 * i + strip - STRIPS)) // OWN_ROWS
            for a in range(2):
                greet((src + a, 1))

    one = ga == 1
    i32 = lambda b: jnp.where(b, jnp.int32(1), jnp.int32(0))
    n_waits = (n_waits + 2 + 2 * i32(crosses)
               + 2 * i32(jnp.logical_and(one, t0 < ANTI))
               + 2 * i32(jnp.logical_and(jnp.logical_and(one, crosses), t0 + 1 < ANTI)))

    own_cols = pl.ds(pl.multiple_of(ga * HALF, BLK), HALF)
    oth_cols = pl.ds(pl.multiple_of((1 - ga) * HALF, BLK), HALF)
    l_w = pltpu.make_async_copy(wt, wraw, s_loc.at[0])
    l_part = pltpu.make_async_copy(part, praw, s_loc.at[1])
    l_pd = pltpu.make_async_copy(pd, pfull.at[:, own_cols], s_loc.at[2])
    l_w.start()
    l_part.start()
    l_pd.start()

    l_w.wait()
    row = lax.broadcasted_iota(jnp.int32, (2 * TILE, TILE), 0)
    col = lax.broadcasted_iota(jnp.int32, (2 * TILE, TILE), 1)
    place = jnp.where(row == col + off, 1.0, 0.0).astype(BF16)
    for b in range(2):
        placed = nn(place, wraw[b]).astype(BF16)
        wplace[b, 0] = placed[:TILE]
        wplace[b, 1] = placed[TILE:]

    @pl.loop(0, ROWS // MC)
    def _(m):
        rows = pl.ds(m * MC, MC)
        for b in range(7):
            acc[b, rows, :] = jnp.zeros((MC, MXU), F32)

    l_part.wait()

    @pl.loop(0, KP // 2)
    def _(kk):
        keep, send = [], []
        for h in range(2):
            k = 2 * kk + h
            both = praw[pl.ds(80 * k, 80), :].astype(F32)
            zero_first = qs[2 * k] == ga
            keep.append(jnp.where(zero_first, both[:40], both[40:]))
            send.append(jnp.where(zero_first, both[40:], both[:40]))
        rows = pl.ds(80 * kk, 80)
        qfull[rows, own_cols] = jnp.concatenate(keep, axis=0).astype(BF16)
        qsend[rows, :] = jnp.concatenate(send, axis=0).astype(BF16)

    pl.semaphore_wait(bar, n_waits)

    p0 = []

    def push0(cond, src, dst, target, sem):
        copy = pltpu.make_async_remote_copy(src, dst, s_p0.at[sem], r_p0, device_id=target, device_id_type=MESH)
        p0.append((cond, copy))

        @pl.when(cond)
        def _():
            copy.start()

    sem = 0
    for tt in range(2):
        t = t0 + tt
        node = (t + SHIFT) % NODES
        slot = ka - (TILE * t) // OWN_ROWS
        cond = crosses if tt else ka >= 0
        for b in range(2):
            push0(cond, wplace.at[b, tt], rbuf.at[slot, ga], (node, b), sem)
            sem += 1
    for tt in range(2):
        t = t0 + tt
        node = (STRIPS + t % 8 + SHIFT) % NODES
        slot = ka - (TILE * t) // OWN_ROWS
        cond = jnp.logical_and(one, t < ANTI)
        if tt:
            cond = jnp.logical_and(cond, crosses)
        lanes = pl.ds(pl.multiple_of(jnp.minimum(t // 8, 6) * BLK, BLK), BLK)
        for b in range(2):
            push0(cond, wplace.at[b, tt, :, lanes], rbuf.at[slot, 1, :, lanes], (node, b), sem)
            sem += 1

    d_p = pltpu.make_async_remote_copy(pd, pfull.at[:, own_cols], s_d2d.at[0], r_d2d.at[0],
                                       device_id=sibling, device_id_type=MESH)
    d_p.start()
    d_q = pltpu.make_async_remote_copy(qsend, qfull.at[:, own_cols], s_d2d.at[1], r_d2d.at[1],
                                       device_id=sibling, device_id_type=MESH)
    d_q.start()

    @pl.when(is_strip)
    def _():
        pltpu.make_async_copy(rbuf, rbuf, r_p0).wait()
        half = [(rbuf[0, h].astype(F32) + rbuf[1, h].astype(F32)).astype(BF16) for h in range(2)]
        dbl[:, 0:HALF] = half[0]
        dbl[:, HALF:2 * HALF] = half[1]
        dbl[:, 2 * HALF:3 * HALF] = half[0]

    @pl.when(is_anti)
    def _():
        pltpu.make_async_copy(rbuf.at[:, 1], rbuf.at[:, 1], r_p0).wait()
        dbl[:, 0:HALF] = (rbuf[0, 1].astype(F32) + rbuf[1, 1].astype(F32)).astype(BF16)

    @pl.when(strip >= STRIPS + 8)
    def _():
        dbl[:, 0:HALF] = jnp.zeros((TILE, HALF), BF16)

    first = jnp.where(is_strip, strip // 8, 0)

    def window(j, n):
        return dbl[:, pl.ds(pl.multiple_of((first + j) * BLK, BLK), n * BLK)]

    m1[z, y, x, :, 0:128] = window(0, 1)
    m2[z, y, x] = window(1, 3)
    m1[z, y, x, :, 128:512] = window(4, 3)

    sends = []

    def push(src, target, ss, rs):
        copy = pltpu.make_async_remote_copy(src, src, ss, rs, device_id=target, device_id_type=MESH)
        copy.start()
        sends.append(copy)
        return copy

    c1 = []
    for d in (1, 2, 3):
        c1.append(push(m1.at[z, y, x], dev(dx=d), s_1.at[d - 1], r_1.at[d - 1]))
        c1.append(push(m2.at[z, y, x], dev(dy=d), s_1.at[d + 2], r_1.at[d + 2]))
    for c in c1:
        c.wait_recv()

    ca = [push(m1.at[z, y, :, :, pl.ds(0, 128)], dev(dy=d), s_a2.at[d - 1], r_a2.at[d - 1]) for d in (1, 2, 3)]

    def line_b(zp, xx):
        return m2.at[zp, :, xx]

    def line_c(zp, yy):
        return m1.at[zp, yy, :, :, pl.ds(128, 384)]

    def plane_a(zp):
        return m1.at[zp, :, :, :, pl.ds(0, 128)]

    zc = {}

    def z_send(dirn, dist, zp, kinds):
        g = 0 if dirn > 0 else 1
        got = zc.setdefault((g, dist), {})
        for kind in kinds:
            n = "abc".index(kind)
            if kind == "a":
                src = plane_a(zp) if dist < 4 else m1.at[zp, pl.ds(2 * g, 2), :, :, pl.ds(0, 128)]
            elif kind == "b":
                src = line_b(zp, x)
            else:
                src = line_c(zp, y)
            idx = (g * 4 + dist - 1) * 3 + n
            got[kind] = push(src, dev(dz=dirn), s_z.at[idx], r_z.at[idx])

    xy1, xy2 = {}, {}

    def xy_send(slot, zp):
        base = slot * 8
        xy1[slot] = [
            push(line_b(zp, x), dev(dx=1), s_xy.at[base], r_xy.at[base]),
            push(line_b(zp, x), dev(dx=-1), s_xy.at[base + 1], r_xy.at[base + 1]),
            push(line_c(zp, y), dev(dy=1), s_xy.at[base + 2], r_xy.at[base + 2]),
            push(line_c(zp, y), dev(dy=-1), s_xy.at[base + 3], r_xy.at[base + 3]),
        ]

    def xy_forward(slot, zp):
        base = slot * 8 + 4
        xl, xr = (x + 3) % NX, (x + 1) % NX
        yl, yr = (y + 3) % NY, (y + 1) % NY
        xy1[slot][0].wait_recv()
        f0 = push(m2.at[zp, pl.ds(0, 2), xl], dev(dx=1), s_xy.at[base], r_xy.at[base])
        xy1[slot][2].wait_recv()
        f2 = push(m1.at[zp, yl, pl.ds(0, 2), :, pl.ds(128, 384)], dev(dy=1), s_xy.at[base + 2], r_xy.at[base + 2])
        xy1[slot][1].wait_recv()
        f1 = push(m2.at[zp, pl.ds(2, 2), xr], dev(dx=-1), s_xy.at[base + 1], r_xy.at[base + 1])
        xy1[slot][3].wait_recv()
        f3 = push(m1.at[zp, yr, pl.ds(2, 2), :, pl.ds(128, 384)], dev(dy=-1), s_xy.at[base + 3], r_xy.at[base + 3])
        xy2[slot] = [f0, f1, f2, f3]

    def at(d):
        return (z + d + NZ) % NZ

    def blk(zp, h, j):
        if j == 0:
            v = m1[zp, 2 * h:2 * h + 2, :, :, 0:128]
        elif j <= 3:
            v = m2[zp, 2 * h:2 * h + 2, :, :, 128 * (j - 1):128 * j]
        else:
            v = m1[zp, 2 * h:2 * h + 2, :, :, 128 * (j - 3):128 * (j - 2)]
        return v.reshape(128, 128)

    def compute(zp):
        i = (zp + NZ - ZSHIFT) % NZ

        @pl.when(i < 7)
        def _():
            upper = blk(zp, 0, 1)
            wn[0:128, 0:128] = blk(zp, 0, 0)
            wn[0:128, 128:256] = upper
            wn[128:256, 0:128] = upper.astype(F32).T.astype(BF16)
            wn[128:256, 128:256] = blk(zp, 1, 0)
            for d in (1, 2, 3):
                wn[0:128, 256 * d:256 * d + 128] = blk(zp, 0, 2 * d)
                if d < 3:
                    wn[0:128, 256 * d + 128:256 * d + 256] = blk(zp, 0, 2 * d + 1)
                else:
                    wn[0:128, 256 * d + 128:256 * d + 256] = jnp.zeros((128, 128), BF16)
                wn[128:256, 256 * d:256 * d + 128] = blk(zp, 1, 2 * d - 1)
                wn[128:256, 256 * d + 128:256 * d + 256] = blk(zp, 1, 2 * d)

            @pl.loop(0, ROWS // MC)
            def _(m):
                rows = pl.ds(m * MC, MC)
                own = pfull[rows, pl.ds(pl.multiple_of(MXU * i, MXU), MXU)]
                for d in (1, 2, 3):
                    j = (i + d) % 7
                    acc[j, rows, :] += nn(own, wn[:, 256 * d:256 * d + 256])
                total = nn(own, wn[:, 0:256])
                for d in (1, 2, 3):
                    j = (i + d) % 7
                    cols = pl.ds(pl.multiple_of(MXU * j, MXU), MXU)
                    total += nt(pfull[rows, cols], wn[:, 256 * d:256 * d + 256])
                acc[i, rows, :] += total

        @pl.when(i == 7)
        def _():
            wn[:, 0:256] = jnp.zeros((256, 256), BF16)
            wn[:, 256:512] = jnp.zeros((256, 256), BF16)
            wn[:, 512:768] = jnp.zeros((256, 256), BF16)
            for b in range(3):
                wn[0:128, 256 * b:256 * b + 128] = blk(zp, 0, 2 * b)
                wn[128:256, 256 * b + 128:256 * b + 256] = blk(zp, 0, 2 * b + 1)
            wn[0:128, 768:896] = blk(zp, 0, 6)

            @pl.loop(0, ROWS // MC)
            def _(m):
                rows = pl.ds(m * MC, MC)
                for b in range(3):
                    w = wn[:, 256 * b:256 * b + 256]
                    r = nn(pfull[rows, 256 * b:256 * b + 256], w)
                    acc[3 + b, rows, 128:256] += r[:, 0:128]
                    acc[4 + b, rows, 0:128] += r[:, 128:256]
                    acc[b, rows, :] += nt(pfull[rows, 896 + 256 * b:896 + 256 * b + 256], w)
                w = wn[0:128, 768:896]
                acc[6, rows, 128:256] += nn(pfull[rows, 768:896], w)
                acc[3, rows, 0:128] += nt(pfull[rows, 1664:1792], w)

    slabs = {0: [(0, 0)], 1: [(1, -1), (2, 1)], 2: [(3, -2), (4, 2)], 3: [(5, -3), (6, 3)], 4: [(7, 4)]}
    z_send(1, 1, z, "bc")
    z_send(-1, 1, z, "bc")
    xy_send(0, z)
    for c in ca:
        c.wait_recv()
    z_send(1, 1, z, "a")
    z_send(-1, 1, z, "a")

    def arrive(dist):
        if dist < 4:
            for slot, delta in slabs[dist]:
                g = 0 if delta < 0 else 1
                dirn = 1 if delta < 0 else -1
                zp = at(delta)
                got = zc[(g, dist)]
                onward = "abc" if dist < 3 else ("ab" if g == 0 else "ac")
                for kind in "bca":
                    got[kind].wait_recv()
                    if kind in onward:
                        z_send(dirn, dist + 1, zp, kind)
                xy_send(slot, zp)
        else:
            zp = at(4)
            zc[(0, 4)]["b"].wait_recv()
            zc[(1, 4)]["c"].wait_recv()
            xy_send(7, zp)
            zc[(0, 4)]["a"].wait_recv()
            zc[(1, 4)]["a"].wait_recv()

    def forward(dist):
        for slot, delta in slabs[dist]:
            xy_forward(slot, at(delta))

    waited = []

    def finish(dist):
        for slot, delta in slabs[dist]:
            for c in xy2[slot]:
                c.wait_recv()
            if not waited:
                waited.append(1)
                l_pd.wait()
                d_p.wait_recv()
            compute(at(delta))

    arrive(1)
    forward(0)
    for dist in range(2, 5):
        arrive(dist)
        forward(dist - 1)
        finish(dist - 2)
    forward(4)
    finish(3)
    finish(4)

    d_q.wait_recv()

    @pl.loop(0, KP // 4)
    def _(a):
        rows = pl.ds(160 * a, 160)
        r = jnp.zeros((160, 160), F32)
        for b in range(7):
            r += nt(acc[b, rows, :].astype(BF16), qfull[rows, 256 * b:256 * b + 256])
        for h in range(4):
            kp[4 * a + h] = r[40 * h:40 * h + 40, 40 * h:40 * h + 40]

    live = cnt[...]
    for p in range(SLOTS):
        v = kp[:, p, :]
        mine[:, 40 * p:40 * p + 40] = jnp.where(live > p, v, 0.0)

    d_o = pltpu.make_async_remote_copy(mine, other, s_d2d.at[2], r_d2d.at[2], device_id=sibling, device_id_type=MESH)
    d_o.start()
    d_o.wait_recv()
    a, b = mine[...], other[...]
    for j in range(2):
        out[j] = jnp.where(qv[:, j:j + 1] == ga, a, b)

    d_o.wait_send()
    d_p.wait_send()
    d_q.wait_send()
    for c in sends:
        c.wait_send()
    for cond, copy in p0:
        @pl.when(cond)
        def _(copy=copy):
            copy.wait_send()


def local(pair_dens, counts, q_index, w_tiles, partner):
    wt = jnp.pad(jnp.transpose(w_tiles, (0, 2, 1)), ((0, 0), (0, TILE - OWN_ROWS), (0, 0)))
    anyspace = pl.BlockSpec(memory_space=pl.ANY)
    vmem = pl.BlockSpec(memory_space=pltpu.VMEM)
    smem = pl.BlockSpec(memory_space=pltpu.SMEM)
    dma = pltpu.SemaphoreType.DMA
    res = pl.pallas_call(
        kernel,
        out_shape=jax.ShapeDtypeStruct((2, KP, SLOTS * PC), F32),
        in_specs=[anyspace, anyspace, anyspace, vmem, vmem, smem],
        out_specs=vmem,
        scratch_shapes=[
            pltpu.VMEM((ROWS, NG), BF16),
            pltpu.VMEM((ROWS, NG), BF16),
            pltpu.VMEM((2 * ROWS, HALF), BF16),
            pltpu.VMEM((ROWS, HALF), BF16),
            pltpu.VMEM((NZ, NY, NX, TILE, 512), BF16),
            pltpu.VMEM((NZ, NY, NX, TILE, 384), BF16),
            pltpu.VMEM((7, ROWS, MXU), F32),
            pltpu.VMEM((2, 2, TILE, HALF), BF16),
            pltpu.VMEM((2, TILE, HALF), BF16),
            pltpu.VMEM((2, 2, TILE, HALF), BF16),
            pltpu.VMEM((TILE, 3 * HALF), BF16),
            pltpu.VMEM((MXU, 4 * MXU), BF16),
            pltpu.VMEM((KP, SLOTS, PC), F32),
            pltpu.VMEM((KP, SLOTS * PC), F32),
            pltpu.VMEM((KP, SLOTS * PC), F32),
            dma((3,)),
            dma((8,)), dma(()),
            dma((3,)), dma((3,)),
            dma((6,)), dma((6,)),
            dma((3,)), dma((3,)),
            dma((24,)), dma((24,)),
            dma((64,)), dma((64,)),
        ],
        compiler_params=pltpu.CompilerParams(
            collective_id=0, has_side_effects=True, vmem_limit_bytes=60 * 2**20),
        cost_estimate=pl.CostEstimate(flops=2 * ROWS * NG * NG, bytes_accessed=8 * 2**20, transcendentals=0),
    )(
        pair_dens.reshape(ROWS, HALF),
        partner.reshape(2 * ROWS, HALF),
        wt,
        counts.reshape(KP, 1),
        q_index,
        q_index.reshape(2 * KP),
    )
    return jnp.transpose(res, (1, 0, 2))


def solution(mesh):
    in_specs = (
        P("ka", None, "ga"),
        P("ka"),
        P("ka", None),
        P(None, "ga", "ka"),
        P("ka", None, None, "ga"),
    )
    return jax.shard_map(local, mesh=mesh, in_specs=in_specs, out_specs=P("ka", None, None), check_vma=False)
```

time: 249 us -> 73.8 us (0.30)
  waiting for transfers between devices: 191 us -> 0 us
  Pallas kernels: 0 us -> 67.3 us
  matrix products: 24.8 us -> 0 us
  between operations: 13.1 us -> 0.01 us
  other arithmetic: 8.86 us -> 0 us
  local copies, waits for them, and re-layouts: 10.9 us -> 6.32 us
    all_gather x1 -> x0, waiting for transfers between devices: 125 us -> none  [local(): lax.all_gather(w_tiles, 'ka', axis=2, tiled=True)]
    pallas_call x0 -> x1, Pallas kernels: none -> 67.3 us  [local(): pl.pallas_call(kernel, out_shape=jax.ShapeDtypeStruct((2, KP, SLOTS * PC)...]
    reduce_scatter x1 -> x0, waiting for transfers between devices: 33 us -> none  [local(): lax.psum_scatter(partial_all, 'ga', scatter_dimension=2, tiled=True)]
    psum x1 -> x0, waiting for transfers between devices: 32.5 us -> none  [local(): summed = lax.psum(chosen, 'ga')]
    dot_general x2 -> x0, matrix products: 24.8 us -> none  [the longest x1 16.3 us: local(): jnp.einsum('rh,bhc->brc', flat_rows, lax.all_gather(w_tiles, 'ka', axis=2...]
    convert_element_type x1 -> x0, local copies, waits for them, and re-layouts: 7.29 us -> none  [local(): lax.psum_scatter(partial_all, 'ga', scatter_dimension=2, tiled=True)]
    convert_element_type x1 -> x0, other arithmetic: 6.14 us -> none  [local(): lax.psum_scatter(partial_all, 'ga', scatter_dimension=2, tiled=True)]
    select_n x1 -> x0, other arithmetic: 2.63 us -> none  [local(): jnp.where(live_mask, summed, jnp.float32(0.0))]
  transfers between devices with their start and end apart: 3 -> 0, of which waited for: 3 -> 0; matrix products, arithmetic and copies ran while one was open for 0% -> 0% of each run, Pallas kernels for 0% -> 0%
where the time goes in v1:
time: 73.8 us; the launch traced here: 73.6 us
  Pallas kernels  67.3 us (91%)
  local copies, waits for them, and re-layouts  6.32 us (9%)
    pallas_call x1, Pallas kernels, local(): pl.pallas_call(kernel, out_shape=jax.ShapeDtypeStruct((2, KP, SLOTS * PC)...  67.3 us
    transpose x1, local copies, waits for them, and re-layouts, local(): return jnp.transpose(res, (1, 0, 2))  2.09 us
    unnamed x4, local copies, waits for them, and re-layouts  1.57 us

profile of v1, /device:TPU:1, one launch (start us, length us, event | category | flops | bytes accessed | tf_op | source)
XLA Modules:
  0.0 73.6 jit_solution(14047147953166041422)
XLA Ops:
  0.0 0.8 %copy.14.qv = s32[32,2]{1,0:T(8,128)S(1)} copy(s32[32,2]{0,1:T(2,128)} %param.7) | data formatting | bytes 512 | tf_op args[2]
  0.8 0.0 copy-start
  0.8 0.7 reshape.15.qs
  1.5 1.3 %copy.13.cnt = s32[32,1]{1,0:T(8,128)} copy(s32[32,1]{0,1:T(1,128)} %bitcast.9) | data formatting | bytes 256 | tf_op jit(solution)/shard_map/reshape | solution.py:458
  2.8 0.8 %copy.17 = bf16[2,896,14]{1,2,0:T(8,128)(2,1)S(1)} copy(bf16[2,896,14]{1,0,2:T(2,128)(2,1)} %param.8) | data formatting | bytes 100352 | tf_op args[3]
  3.6 0.6 pad.4.wt
  4.2 0.0 copy-done
  4.2 67.3 %shard_map.55 = f32[2,32,1600]{2,1,0:T(8,128)} custom-call(bf16[1280,896]{1,0:T(8,128)(2,1)} %bitcast.11, bf16[2560,896]{1,0:T(8,128)(2,1)} %bitcast.10, bf16[2,16,896]{2,1,0:T(8,128)(2,1)} %pad.4.wt, s32[32,1]{1,0:T(8,128)} %copy.13.cnt, s32[32,2]{1,0:T(8,128)} %copy-done, s32[64]{0:T(128)} %reshape.15.qs), custom_call_target="tpu_custom_call" | custom-call | flops 8220835840 | bytes 8388608 | tf_op jit(solution)/shard_map/pallas_call | solution.py:422
  71.5 2.1 %copy.15 = f32[32,2,1600]{2,1,0:T(2,128)} copy(f32[32,2,1600]{2,0,1:T(8,128)} %bitcast.7) | data formatting | bytes 819200 | tf_op jit(solution)/shard_map/transpose | solution.py:462
Async XLA Ops:
  0.8 3.5 %copy-start = (s32[32,2]{1,0:T(8,128)}, s32[32,2]{1,0:T(8,128)S(1)}, u32[]{:S(2)}) copy-start(s32[32,2]{1,0:T(8,128)S(1)} %copy.14.qv) | copy-start | bytes 772

commit v2 on v0

v2 whole, which is shorter than its diff:
```python
import jax
import jax.numpy as jnp
from jax import lax
from jax.experimental import pallas as pl
from jax.experimental.pallas import tpu as pltpu
from jax.sharding import PartitionSpec as P

MESH = pl.DeviceIdType.MESH
BF16, F32 = jnp.bfloat16, jnp.float32

NX, NY, NZ = 4, 4, 8
NODES = NX * NY * NZ
KP, SLOTS, PC = 32, 40, 40
ROWS = KP * SLOTS
NG, HALF = 1792, 896
BLK, MXU = 128, 256
OWN_ROWS = NG // NODES
TILE = 16
STRIPS = NG // TILE
SLAB = NX * NY
WIN = 8
MC = 256


def nt(a, b):
    return lax.dot_general(a, b, (((1,), (1,)), ((), ())), preferred_element_type=F32)


def nn(a, b):
    return jnp.dot(a, b, preferred_element_type=F32)


def kernel(pd, part, wt, cnt_in, q_in, out,
           cnt, qs, pfull, qfull, praw, qsend, ma, mb, mc, acc, rbuf, wraw, wplace, wn, kp, mine, other,
           s_loc, s_p0, r_p0, s_d2d, r_d2d, s_1, r_1, s_a, r_a, s_z, r_z, s_xy, r_xy):
    ka = lax.axis_index("ka")
    ga = lax.axis_index("ga")
    x, y, z = ka % NX, (ka // NX) % NY, ka // (NX * NY)

    def dev(dz=0, dy=0, dx=0):
        return (((z + dz + NZ) % NZ) * (NX * NY) + ((y + dy + NY) % NY) * NX + (x + dx + NX) % NX, ga)

    sibling = (ka, 1 - ga)
    has_strip = ka < STRIPS

    bar = pltpu.get_barrier_semaphore()

    def greet(device):
        pl.semaphore_signal(bar, inc=1, device_id=device, device_id_type=MESH)

    i32 = lambda b: jnp.where(b, jnp.int32(1), jnp.int32(0))

    t0 = (OWN_ROWS * ka) // TILE
    off = (OWN_ROWS * ka) % TILE
    crosses = off + OWN_ROWS > TILE
    n_waits = jnp.int32(14)
    for d in (1, 2, 3):
        greet(dev(dx=d))
        greet(dev(dy=d))
    for d in range(1, NZ):
        greet(dev(dz=d))
    greet(sibling)

    first_src = (TILE * ka) // OWN_ROWS
    for a in range(2):
        for c in range(2):
            @pl.when(jnp.logical_and(has_strip, jnp.logical_or(first_src + a != ka, ga != c)))
            def _(a=a, c=c):
                greet((first_src + a, c))

    n_waits += (2 - i32(t0 == ka)) + i32(crosses) * (2 - i32(t0 + 1 == ka))

    own_cols = pl.ds(pl.multiple_of(ga * HALF, BLK), HALF)
    l_w = pltpu.make_async_copy(wt, wraw, s_loc.at[0])
    l_part = pltpu.make_async_copy(part, praw, s_loc.at[1])
    l_pd = pltpu.make_async_copy(pd, pfull.at[:, own_cols], s_loc.at[2])
    l_cnt = pltpu.make_async_copy(cnt_in, cnt, s_loc.at[3])
    l_q = pltpu.make_async_copy(q_in, qs, s_loc.at[4])
    l_w.start()
    l_cnt.start()
    l_q.start()
    l_part.start()
    l_pd.start()

    l_w.wait()
    row = lax.broadcasted_iota(jnp.int32, (2 * TILE, OWN_ROWS), 0)
    col = lax.broadcasted_iota(jnp.int32, (2 * TILE, OWN_ROWS), 1)
    place = jnp.where(row == col + off, 1.0, 0.0).astype(BF16)
    raw = wraw[...].astype(F32)
    for b in range(2):
        placed = nn(place, raw[:, b, :].astype(BF16)).astype(BF16)
        wplace[b, 0] = placed[:TILE]
        wplace[b, 1] = placed[TILE:]

    pl.semaphore_wait(bar, n_waits)

    p0 = []

    def push0(cond, src, dst, node, b, sem):
        copy = pltpu.make_async_remote_copy(src, dst, s_p0.at[sem], r_p0, device_id=(node, b), device_id_type=MESH)
        here = jnp.logical_and(node == ka, ga == b)
        away = jnp.logical_and(cond, jnp.logical_not(here))
        p0.append((away, copy))

        @pl.when(away)
        def _():
            copy.start()

        @pl.when(jnp.logical_and(cond, here))
        def _():
            pltpu.make_async_copy(src, dst, r_p0).start()

    sem = 0
    for tt in range(2):
        t = t0 + tt
        slot = ka - (TILE * t) // OWN_ROWS
        lead = (t // 8) % 7
        same = (t // 8) // 7 == ga
        start = jnp.where(same, lead, 0)
        shift = jnp.where(same, 0, 7 - lead)
        count = jnp.where(same, 7 - lead, lead + 1)
        for size in (4, 2, 1):
            cond = (count // size) % 2 == 1
            if tt:
                cond = jnp.logical_and(cond, crosses)
            more = (count // (2 * size)) * (2 * size)
            begin = jnp.minimum(start + more, 7 - size)
            to = jnp.minimum(shift + more, WIN - size)
            src = pl.ds(pl.multiple_of(begin * BLK, BLK), size * BLK)
            dst = pl.ds(pl.multiple_of(to * BLK, BLK), size * BLK)
            for b in range(2):
                push0(cond, wplace.at[b, tt, :, src], rbuf.at[slot, :, dst], t, b, sem)
                sem += 1

    d_p = pltpu.make_async_remote_copy(pd, pfull.at[:, own_cols], s_d2d.at[0], r_d2d.at[0],
                                       device_id=sibling, device_id_type=MESH)
    d_p.start()
    l_cnt.wait()
    l_q.wait()
    l_part.wait()

    @pl.loop(0, KP // 2)
    def _(kk):
        keep, send = [], []
        for h in range(2):
            k = 2 * kk + h
            both = praw[pl.ds(80 * k, 80), :].astype(F32)
            zero_first = qs[0, k] == ga
            keep.append(jnp.where(zero_first, both[:40], both[40:]))
            send.append(jnp.where(zero_first, both[40:], both[:40]))
        rows = pl.ds(80 * kk, 80)
        qfull[rows, own_cols] = jnp.concatenate(keep, axis=0).astype(BF16)
        qsend[rows, :] = jnp.concatenate(send, axis=0).astype(BF16)

    d_q = pltpu.make_async_remote_copy(qsend, qfull.at[:, own_cols], s_d2d.at[1], r_d2d.at[1],
                                       device_id=sibling, device_id_type=MESH)
    d_q.start()

    @pl.loop(0, ROWS // MC)
    def _(m):
        rows = pl.ds(m * MC, MC)
        for b in range(7):
            acc[b, rows, :] = jnp.zeros((MC, MXU), F32)

    @pl.when(has_strip)
    def _():
        pltpu.make_async_copy(rbuf, rbuf, r_p0).wait()
        whole = (rbuf[0].astype(F32) + rbuf[1].astype(F32)).astype(BF16)
        ma[z, y, x] = whole[:, 0:128]
        mb[z, y, x, :, 0:384] = whole[:, 128:512]
        mc[z, y, x] = whole[:, 512:896]
        mb[z, y, x, :, 384:512] = whole[:, 896:1024]

    sends = []

    def drain(sem, elements):
        lanes = 256 if elements > ROWS * 128 else 128
        ref = qsend.at[pl.ds(0, elements // lanes), pl.ds(0, lanes)]
        pltpu.make_async_copy(ref, ref, sem).wait()

    def push(zp, src, target, ss, rs):
        copy = pltpu.make_async_remote_copy(src, src, ss, rs, device_id=target, device_id_type=MESH)

        @pl.when(zp != NZ - 1)
        def _():
            copy.start()

    def arrive(zp, sem, elements):
        @pl.when(zp != NZ - 1)
        def _():
            drain(sem, elements)

    for d in (1, 2, 3):
        push(z, mb.at[z, y, x], dev(dy=d), s_1, r_1.at[0])
    for d in (1, 2, 3):
        push(z, mc.at[z, y, x], dev(dx=d), s_1, r_1.at[1])
    for d in range(1, NZ):
        push(z, ma.at[z, y, x], dev(dz=d), s_1, r_a.at[0])
    sends.append((z, s_1, TILE * (3 * 512 + 3 * 384 + 7 * 128)))

    B0, B1, C0 = 2 * TILE * 512, 2 * TILE * 384, 4 * TILE * 384

    def line_b(zp, xx, n):
        return mb.at[zp, pl.ds(0, 2), xx] if n == 0 else mb.at[zp, pl.ds(2, 2), xx, :, pl.ds(0, 384)]

    def z_send(g, dist, zp, kind):
        hop = (1 if dist < 4 else 2) * (1 if g == 0 else -1)
        srcs = [line_b(zp, x, 0), line_b(zp, x, 1)] if kind == "b" else [mc.at[zp, y]]
        n = g * 4 + dist - 1
        for src in srcs:
            push(zp, src, dev(dz=hop), s_z.at[n], r_z.at[2 * n + "bc".index(kind)])
        if dist < 4 and kind == "b":
            sends.append((zp, s_z.at[n], B0 + B1 + C0))
        elif dist == 4:
            sends.append((zp, s_z.at[n], B0 + B1 if kind == "b" else C0))

    def z_arrive(g, dist, zp, kind):
        arrive(zp, r_z.at[2 * (g * 4 + dist - 1) + "bc".index(kind)], B0 + B1 if kind == "b" else C0)

    def xy_send(slot, zp, kind):
        s, r = s_xy.at[slot], 5 * slot
        if kind == "b":
            push(zp, line_b(zp, x, 0), dev(dx=1), s, r_xy.at[r])
            push(zp, line_b(zp, x, 1), dev(dx=-1), s, r_xy.at[r + 1])
            push(zp, line_b(zp, x, 1), dev(dx=1), s, r_xy.at[r + 4])
            push(zp, line_b(zp, x, 0), dev(dx=-1), s, r_xy.at[r + 4])
        else:
            push(zp, mc.at[zp, y], dev(dy=1), s, r_xy.at[r + 2])
            push(zp, mc.at[zp, y], dev(dy=-1), s, r_xy.at[r + 3])
            sends.append((zp, s, 3 * (B0 + B1) + 3 * C0))

    def xy_forward(slot, zp):
        xl, xr = (x + 3) % NX, (x + 1) % NX
        yl, yr = (y + 3) % NY, (y + 1) % NY
        todo = [
            (B0, line_b(zp, xl, 0), dev(dx=1)),
            (B1, line_b(zp, xr, 1), dev(dx=-1)),
            (C0, mc.at[zp, yl, pl.ds(0, 2)], dev(dy=1)),
            (C0, mc.at[zp, yr, pl.ds(2, 2)], dev(dy=-1)),
        ]
        for n, (size, src, target) in enumerate(todo):
            arrive(zp, r_xy.at[5 * slot + n], size)
            push(zp, src, target, s_xy.at[slot], r_xy.at[5 * slot + 4])

    def at(d):
        return (z + d + NZ) % NZ

    SLOT = {0: 0, -1: 1, 1: 2, -2: 3, 2: 4, -3: 5, 3: 6, 4: 7}

    def z_step(dist, kind):
        if dist == 4:
            z_arrive(0 if kind == "b" else 1, 4, at(4), kind)
            xy_send(7, at(4), kind)
            return
        for g in (0, 1):
            delta = -dist if g == 0 else dist
            z_arrive(g, dist, at(delta), kind)
            if dist < 3:
                z_send(g, dist + 1, at(delta), kind)
            if dist == 2 and kind == "bc"[g]:
                z_send(g, 4, at(delta), kind)
            xy_send(SLOT[delta], at(delta), kind)

    def blk(zp, h, j):
        ref, lane = (ma, 0) if j == 0 else (mb, min(j - 1, 3)) if j <= 3 or j == 7 else (mc, j - 4)
        return ref[zp, 2 * h:2 * h + 2, :, :, 128 * lane:128 * lane + 128].reshape(128, 128)

    def compute(i):
        zp = i

        @pl.when(i < NZ - 1)
        def _():
            upper = blk(zp, 0, 1)
            wn[0:128, 0:128] = blk(zp, 0, 0)
            wn[0:128, 128:256] = upper
            wn[128:256, 0:128] = upper.astype(F32).T.astype(BF16)
            wn[128:256, 128:256] = blk(zp, 1, 0)
            for d in (1, 2, 3):
                wn[0:128, 256 * d:256 * d + 128] = blk(zp, 0, 2 * d)
                wn[0:128, 256 * d + 128:256 * d + 256] = blk(zp, 0, 2 * d + 1)
                wn[128:256, 256 * d:256 * d + 128] = blk(zp, 1, 2 * d - 1)
                wn[128:256, 256 * d + 128:256 * d + 256] = blk(zp, 1, 2 * d)

            own = pfull[:, pl.ds(pl.multiple_of(MXU * i, MXU), MXU)]
            for d in (1, 2, 3):
                acc[(i + d) % 7] += nn(own, wn[:, 256 * d:256 * d + 256])
            total = nn(own, wn[:, 0:256])
            for d in (1, 2, 3):
                cols = pl.ds(pl.multiple_of(MXU * ((i + d) % 7), MXU), MXU)
                total += nt(pfull[:, cols], wn[:, 256 * d:256 * d + 256])
            acc[i] += total

    def forward(dist):
        for delta in ((0,) if dist == 0 else (4,) if dist == 4 else (-dist, dist)):
            xy_forward(SLOT[delta], at(delta))

    def finish(dist):
        for delta in ((0,) if dist == 0 else (4,) if dist == 4 else (-dist, dist)):
            arrive(at(delta), r_xy.at[5 * SLOT[delta] + 4], 2 * (B0 + B1) + C0)
        if dist in (0, 4):
            compute(at(dist))
        else:
            @pl.loop(0, 2)
            def _(n):
                compute(at((2 * n - 1) * dist))

    arrive(z, r_1.at[0], 3 * TILE * 512)
    for g in (0, 1):
        z_send(g, 1, z, "b")
    xy_send(0, z, "b")
    arrive(z, r_1.at[1], 3 * TILE * 384)
    for g in (0, 1):
        z_send(g, 1, z, "c")
    xy_send(0, z, "c")

    A0 = 7 * TILE * 128

    def push_a(src, target, n, m):
        pltpu.make_async_remote_copy(src, src, s_a.at[n], r_a.at[m], device_id=target,
                                     device_id_type=MESH).start()

    @pl.when(z == NZ - 1)
    def _():
        drain(r_a.at[0], A0)

    @pl.when(z != NZ - 1)
    def _():
        drain(r_a.at[0], 6 * TILE * 128)

    for d in (1, 2, 3):
        push_a(ma.at[pl.ds(0, 7), y, x], dev(dx=d), 0, 1)
    z_step(1, "b")
    drain(r_a.at[1], 3 * A0)
    push_a(ma.at[pl.ds(0, 7), y], dev(dy=1), 1, 2)
    push_a(ma.at[pl.ds(0, 7), y], dev(dy=-1), 1, 3)
    z_step(1, "c")
    forward(0)
    z_step(2, "b")
    z_step(2, "c")
    drain(r_a.at[2], 4 * A0)
    push_a(ma.at[pl.ds(0, 7), (y + 3) % NY, pl.ds(0, 2)], dev(dy=1), 1, 4)
    drain(r_a.at[3], 4 * A0)
    push_a(ma.at[pl.ds(0, 7), (y + 1) % NY, pl.ds(2, 2)], dev(dy=-1), 1, 4)
    forward(1)
    z_step(3, "b")
    z_step(3, "c")
    z_step(4, "b")
    z_step(4, "c")
    drain(r_a.at[4], 4 * A0)
    l_pd.wait()
    d_p.wait_recv()
    finish(0)
    forward(2)
    finish(1)
    forward(3)
    forward(4)
    finish(2)
    finish(3)
    finish(4)

    d_q.wait_recv()

    @pl.loop(0, KP // 4, unroll=True)
    def _(a):
        rows = pl.ds(160 * a, 160)
        scr = jnp.concatenate([acc[b, rows, :].astype(BF16) for b in range(7)], axis=1)
        r = nt(scr, qfull[rows, :])
        for h in range(4):
            slot = lax.broadcasted_iota(jnp.int32, (SLOTS, PC), 0)
            block = r[40 * h:40 * h + 40, 40 * h:40 * h + 40]
            kp[4 * a + h] = jnp.where(slot < cnt[4 * a + h], block, 0.0)

    for p in range(SLOTS):
        mine[:, 40 * p:40 * p + 40] = kp[:, p, :]

    d_o = pltpu.make_async_remote_copy(mine, other, s_d2d.at[2], r_d2d.at[2], device_id=sibling, device_id_type=MESH)
    d_o.start()

    d_p.wait_send()
    d_q.wait_send()
    drain(s_a.at[0], 3 * A0)
    drain(s_a.at[1], 12 * A0)
    for zp, sem, elements in sends:
        arrive(zp, sem, elements)
    for cond, copy in p0:
        @pl.when(cond)
        def _(copy=copy):
            copy.wait_send()

    d_o.wait_recv()
    point = lax.broadcasted_iota(jnp.int32, (KP, 1), 0)
    first_tile = jnp.zeros((KP, 1), jnp.int32)
    for k in range(KP):
        first_tile = jnp.where(point == k, qs[0, k], first_tile)
    a, b = mine[...], other[...]
    out[0] = jnp.where(first_tile == ga, a, b)
    out[1] = jnp.where(first_tile == ga, b, a)
    d_o.wait_send()


def local(pair_dens, counts, q_index, w_tiles, partner):
    anyspace = pl.BlockSpec(memory_space=pl.ANY)
    vmem = pl.BlockSpec(memory_space=pltpu.VMEM)
    dma = pltpu.SemaphoreType.DMA
    res = pl.pallas_call(
        kernel,
        out_shape=jax.ShapeDtypeStruct((2, KP, SLOTS * PC), F32),
        in_specs=[anyspace] * 5,
        out_specs=vmem,
        scratch_shapes=[
            pltpu.SMEM((KP,), jnp.int32),
            pltpu.SMEM((2, KP), jnp.int32),
            pltpu.VMEM((ROWS, NG), BF16),
            pltpu.VMEM((ROWS, NG), BF16),
            pltpu.VMEM((2 * ROWS, HALF), BF16),
            pltpu.VMEM((ROWS, HALF), BF16),
            pltpu.VMEM((NZ, NY, NX, TILE, 128), BF16),
            pltpu.VMEM((NZ, NY, NX, TILE, 512), BF16),
            pltpu.VMEM((NZ, NY, NX, TILE, 384), BF16),
            pltpu.VMEM((7, ROWS, MXU), F32),
            pltpu.VMEM((2, TILE, WIN * BLK), BF16),
            pltpu.VMEM((OWN_ROWS, 2, HALF), BF16),
            pltpu.VMEM((2, 2, TILE, HALF), BF16),
            pltpu.VMEM((MXU, 4 * MXU), BF16),
            pltpu.VMEM((KP, SLOTS, PC), F32),
            pltpu.VMEM((KP, SLOTS * PC), F32),
            pltpu.VMEM((KP, SLOTS * PC), F32),
            dma((5,)),
            dma((12,)), dma(()),
            dma((3,)), dma((3,)),
            dma(()), dma((2,)),
            dma((2,)), dma((5,)),
            dma((8,)), dma((16,)),
            dma((8,)), dma((40,)),
        ],
        compiler_params=pltpu.CompilerParams(
            collective_id=0, has_side_effects=True, vmem_limit_bytes=60 * 2**20),
        cost_estimate=pl.CostEstimate(flops=2 * ROWS * NG * NG, bytes_accessed=8 * 2**20, transcendentals=0),
    )(
        pair_dens.reshape(ROWS, HALF),
        partner.reshape(2 * ROWS, HALF),
        jnp.transpose(w_tiles, (2, 0, 1)),
        counts,
        jnp.transpose(q_index),
    )
    return jnp.transpose(res, (1, 0, 2))


def solution(mesh):
    in_specs = (
        P("ka", None, "ga"),
        P("ka"),
        P("ka", None),
        P(None, "ga", "ka"),
        P("ka", None, None, "ga"),
    )
    return jax.shard_map(local, mesh=mesh, in_specs=in_specs, out_specs=P("ka", None, None), check_vma=False)
```

time: 249 us -> 54.6 us (0.22)
  waiting for transfers between devices: 191 us -> 0 us
  Pallas kernels: 0 us -> 52.4 us
  matrix products: 24.8 us -> 0 us
  between operations: 13.1 us -> 0.01 us
  other arithmetic: 8.86 us -> 0 us
  local copies, waits for them, and re-layouts: 10.9 us -> 2.09 us
    all_gather x1 -> x0, waiting for transfers between devices: 125 us -> none  [local(): lax.all_gather(w_tiles, 'ka', axis=2, tiled=True)]
    pallas_call x0 -> x1, Pallas kernels: none -> 52.4 us  [local(): pl.pallas_call(kernel, out_shape=jax.ShapeDtypeStruct((2, KP, SLOTS * PC)...]
    reduce_scatter x1 -> x0, waiting for transfers between devices: 33 us -> none  [local(): lax.psum_scatter(partial_all, 'ga', scatter_dimension=2, tiled=True)]
    psum x1 -> x0, waiting for transfers between devices: 32.5 us -> none  [local(): summed = lax.psum(chosen, 'ga')]
    dot_general x2 -> x0, matrix products: 24.8 us -> none  [the longest x1 16.3 us: local(): jnp.einsum('rh,bhc->brc', flat_rows, lax.all_gather(w_tiles, 'ka', axis=2...]
    convert_element_type x1 -> x0, local copies, waits for them, and re-layouts: 7.29 us -> none  [local(): lax.psum_scatter(partial_all, 'ga', scatter_dimension=2, tiled=True)]
    convert_element_type x1 -> x0, other arithmetic: 6.14 us -> none  [local(): lax.psum_scatter(partial_all, 'ga', scatter_dimension=2, tiled=True)]
    reshape x1 -> x0, local copies, waits for them, and re-layouts: 2.93 us -> none  [local(): jnp.where(live_mask, summed, jnp.float32(0.0))]
  transfers between devices with their start and end apart: 3 -> 0, of which waited for: 3 -> 0; matrix products, arithmetic and copies ran while one was open for 0% -> 0% of each run, Pallas kernels for 0% -> 0%
where the time goes in v2:
time: 54.6 us; the launch traced here: 54.5 us
  Pallas kernels  52.4 us (96%)
  local copies, waits for them, and re-layouts  2.09 us (4%)
    pallas_call x1, Pallas kernels, local(): pl.pallas_call(kernel, out_shape=jax.ShapeDtypeStruct((2, KP, SLOTS * PC)...  52.4 us
    transpose x1, local copies, waits for them, and re-layouts, local(): return jnp.transpose(res, (1, 0, 2))  2.09 us

profile of v2, /device:TPU:1, one launch (start us, length us, event | category | flops | bytes accessed | tf_op | source)
XLA Modules:
  0.0 54.5 jit_solution(12001477228103014430)
XLA Ops:
  0.0 52.4 %shard_map.55 = f32[2,32,1600]{2,1,0:T(8,128)} custom-call(bf16[1280,896]{1,0:T(8,128)(2,1)} %bitcast.7, bf16[2560,896]{1,0:T(8,128)(2,1)} %bitcast.6, bf16[14,2,896]{2,1,0:T(2,128)(2,1)} %bitcast.8, s32[32]{0:T(128)} %cnt_in.1, s32[2,32]{1,0:T(2,128)} %bitcast.9), custom_call_target="tpu_custom_call" | custom-call | flops 8220835840 | bytes 8388608 | tf_op jit(solution)/shard_map/pallas_call | solution.py:405
  52.4 2.1 %copy.6 = f32[32,2,1600]{2,1,0:T(2,128)} copy(f32[32,2,1600]{2,0,1:T(8,128)} %bitcast.5) | data formatting | bytes 819200 | tf_op jit(solution)/shard_map/transpose | solution.py:446

commit v3 on v2

--- a/solution.py
+++ b/solution.py
@@ -17,7 +17,8 @@
 OWN_ROWS = NG // NODES
 TILE = 16
 STRIPS = NG // TILE
-SLAB = NX * NY
+SLABS = 7
+EMPTY = NZ // 2
 WIN = 8
 MC = 256
 
@@ -35,40 +36,56 @@
            s_loc, s_p0, r_p0, s_d2d, r_d2d, s_1, r_1, s_a, r_a, s_z, r_z, s_xy, r_xy):
     ka = lax.axis_index("ka")
     ga = lax.axis_index("ga")
-    x, y, z = ka % NX, (ka // NX) % NY, ka // (NX * NY)
-
-    def dev(dz=0, dy=0, dx=0):
-        return (((z + dz + NZ) % NZ) * (NX * NY) + ((y + dy + NY) % NY) * NX + (x + dx + NX) % NX, ga)
+    z = ka // (NX * NY)
+    x_here, y_here = ka % NX, (ka // NX) % NY
+    u = jnp.where(ga == 0, x_here, y_here)
+    v = jnp.where(ga == 0, y_here, x_here)
+
+    def node_of(core, zz, vv, uu):
+        return zz * (NX * NY) + jnp.where(core == 0, vv * NX + uu, uu * NX + vv)
+
+    def dev(dz=0, dv=0, du=0):
+        return (node_of(ga, (z + dz + NZ) % NZ, (v + dv + NY) % NY, (u + du + NX) % NX), ga)
 
     sibling = (ka, 1 - ga)
-    has_strip = ka < STRIPS
+    i32 = lambda b: jnp.where(b, jnp.int32(1), jnp.int32(0))
+
+    def slab_of(zp):
+        return zp - i32(zp > EMPTY)
+
+    def owner(t, core):
+        slab = t // (NX * NY)
+        return node_of(core, slab + i32(slab >= EMPTY), (t // NX) % NY, t % NX)
+
+    has_strip = z != EMPTY
+    me = slab_of(z)
+    strip = me * (NX * NY) + v * NX + u
 
     bar = pltpu.get_barrier_semaphore()
 
     def greet(device):
         pl.semaphore_signal(bar, inc=1, device_id=device, device_id_type=MESH)
-
-    i32 = lambda b: jnp.where(b, jnp.int32(1), jnp.int32(0))
 
     t0 = (OWN_ROWS * ka) // TILE
     off = (OWN_ROWS * ka) % TILE
     crosses = off + OWN_ROWS > TILE
-    n_waits = jnp.int32(14)
+    n_waits = jnp.int32(26)
     for d in (1, 2, 3):
-        greet(dev(dx=d))
-        greet(dev(dy=d))
+        for dz in (0, -1, 1):
+            greet(dev(dz, 0, d))
+            greet(dev(dz, d, 0))
     for d in range(1, NZ):
         greet(dev(dz=d))
     greet(sibling)
 
-    first_src = (TILE * ka) // OWN_ROWS
+    first_src = (TILE * strip) // OWN_ROWS
     for a in range(2):
         for c in range(2):
             @pl.when(jnp.logical_and(has_strip, jnp.logical_or(first_src + a != ka, ga != c)))
             def _(a=a, c=c):
                 greet((first_src + a, c))
 
-    n_waits += (2 - i32(t0 == ka)) + i32(crosses) * (2 - i32(t0 + 1 == ka))
+    n_waits += (2 - i32(owner(t0, ga) == ka)) + i32(crosses) * (2 - i32(owner(t0 + 1, ga) == ka))
 
     own_cols = pl.ds(pl.multiple_of(ga * HALF, BLK), HALF)
     l_w = pltpu.make_async_copy(wt, wraw, s_loc.at[0])
@@ -129,7 +146,7 @@
             src = pl.ds(pl.multiple_of(begin * BLK, BLK), size * BLK)
             dst = pl.ds(pl.multiple_of(to * BLK, BLK), size * BLK)
             for b in range(2):
-                push0(cond, wplace.at[b, tt, :, src], rbuf.at[slot, :, dst], t, b, sem)
+                push0(cond, wplace.at[b, tt, :, src], rbuf.at[slot, :, dst], owner(t, b), b, sem)
                 sem += 1
 
     d_p = pltpu.make_async_remote_copy(pd, pfull.at[:, own_cols], s_d2d.at[0], r_d2d.at[0],
@@ -166,46 +183,52 @@
     def _():
         pltpu.make_async_copy(rbuf, rbuf, r_p0).wait()
         whole = (rbuf[0].astype(F32) + rbuf[1].astype(F32)).astype(BF16)
-        ma[z, y, x] = whole[:, 0:128]
-        mb[z, y, x, :, 0:384] = whole[:, 128:512]
-        mc[z, y, x] = whole[:, 512:896]
-        mb[z, y, x, :, 384:512] = whole[:, 896:1024]
+        ma[me, v, u] = whole[:, 0:128]
+        mb[me, v, u, :, 0:384] = whole[:, 128:512]
+        mc[me, v, u] = whole[:, 512:896]
+        mb[me, v, u, :, 384:512] = whole[:, 896:1024]
 
     sends = []
 
     def drain(sem, elements):
-        lanes = 256 if elements > ROWS * 128 else 128
+        lanes = 128 if elements <= ROWS * 128 else 256 if elements <= ROWS * 256 else HALF
         ref = qsend.at[pl.ds(0, elements // lanes), pl.ds(0, lanes)]
         pltpu.make_async_copy(ref, ref, sem).wait()
 
     def push(zp, src, target, ss, rs):
         copy = pltpu.make_async_remote_copy(src, src, ss, rs, device_id=target, device_id_type=MESH)
 
-        @pl.when(zp != NZ - 1)
+        @pl.when(zp != EMPTY)
         def _():
             copy.start()
 
     def arrive(zp, sem, elements):
-        @pl.when(zp != NZ - 1)
+        @pl.when(zp != EMPTY)
         def _():
             drain(sem, elements)
 
     for d in (1, 2, 3):
-        push(z, mb.at[z, y, x], dev(dy=d), s_1, r_1.at[0])
+        push(z, mb.at[me, v, u], dev(dv=d), s_1, r_1.at[0])
     for d in (1, 2, 3):
-        push(z, mc.at[z, y, x], dev(dx=d), s_1, r_1.at[1])
+        push(z, mc.at[me, v, u], dev(du=d), s_1, r_1.at[1])
     for d in range(1, NZ):
-        push(z, ma.at[z, y, x], dev(dz=d), s_1, r_a.at[0])
-    sends.append((z, s_1, TILE * (3 * 512 + 3 * 384 + 7 * 128)))
+        push(z, ma.at[me, v, u], dev(dz=d), s_1, r_a.at[0])
+    for g, dz in ((0, 1), (1, -1)):
+        for d in range(4):
+            push(z, mb.at[me, v, u], dev(dz, d, 0), s_1, r_z.at[8 * g])
+    for g, dz in ((0, 1), (1, -1)):
+        for d in range(4):
+            push(z, mc.at[me, v, u], dev(dz, 0, d), s_1, r_z.at[8 * g + 1])
+    sends.append((z, s_1, TILE * (11 * 512 + 11 * 384 + 7 * 128)))
 
     B0, B1, C0 = 2 * TILE * 512, 2 * TILE * 384, 4 * TILE * 384
 
-    def line_b(zp, xx, n):
-        return mb.at[zp, pl.ds(0, 2), xx] if n == 0 else mb.at[zp, pl.ds(2, 2), xx, :, pl.ds(0, 384)]
+    def line_b(zp, uu, n):
+        return mb.at[slab_of(zp), pl.ds(0, 2), uu] if n == 0 else mb.at[slab_of(zp), pl.ds(2, 2), uu, :, pl.ds(0, 384)]
 
     def z_send(g, dist, zp, kind):
         hop = (1 if dist < 4 else 2) * (1 if g == 0 else -1)
-        srcs = [line_b(zp, x, 0), line_b(zp, x, 1)] if kind == "b" else [mc.at[zp, y]]
+        srcs = [line_b(zp, u, 0), line_b(zp, u, 1)] if kind == "b" else [mc.at[slab_of(zp), v]]
         n = g * 4 + dist - 1
         for src in srcs:
             push(zp, src, dev(dz=hop), s_z.at[n], r_z.at[2 * n + "bc".index(kind)])
@@ -215,32 +238,34 @@
             sends.append((zp, s_z.at[n], B0 + B1 if kind == "b" else C0))
 
     def z_arrive(g, dist, zp, kind):
+        if dist == 1:
+            arrive(zp, r_z.at[8 * g + "bc".index(kind)], 4 * TILE * (512 if kind == "b" else 384))
+            return
         arrive(zp, r_z.at[2 * (g * 4 + dist - 1) + "bc".index(kind)], B0 + B1 if kind == "b" else C0)
 
     def xy_send(slot, zp, kind):
-        s, r = s_xy.at[slot], 5 * slot
+        s, r = s_xy, 5 * slot
         if kind == "b":
-            push(zp, line_b(zp, x, 0), dev(dx=1), s, r_xy.at[r])
-            push(zp, line_b(zp, x, 1), dev(dx=-1), s, r_xy.at[r + 1])
-            push(zp, line_b(zp, x, 1), dev(dx=1), s, r_xy.at[r + 4])
-            push(zp, line_b(zp, x, 0), dev(dx=-1), s, r_xy.at[r + 4])
+            push(zp, line_b(zp, u, 0), dev(du=1), s, r_xy.at[r])
+            push(zp, line_b(zp, u, 1), dev(du=-1), s, r_xy.at[r + 1])
+            push(zp, line_b(zp, u, 1), dev(du=1), s, r_xy.at[r + 4])
+            push(zp, line_b(zp, u, 0), dev(du=-1), s, r_xy.at[r + 4])
         else:
-            push(zp, mc.at[zp, y], dev(dy=1), s, r_xy.at[r + 2])
-            push(zp, mc.at[zp, y], dev(dy=-1), s, r_xy.at[r + 3])
-            sends.append((zp, s, 3 * (B0 + B1) + 3 * C0))
+            push(zp, mc.at[slab_of(zp), v], dev(dv=1), s, r_xy.at[r + 2])
+            push(zp, mc.at[slab_of(zp), v], dev(dv=-1), s, r_xy.at[r + 3])
 
     def xy_forward(slot, zp):
-        xl, xr = (x + 3) % NX, (x + 1) % NX
-        yl, yr = (y + 3) % NY, (y + 1) % NY
+        ul, ur = (u + 3) % NX, (u + 1) % NX
+        vl, vr = (v + 3) % NY, (v + 1) % NY
         todo = [
-            (B0, line_b(zp, xl, 0), dev(dx=1)),
-            (B1, line_b(zp, xr, 1), dev(dx=-1)),
-            (C0, mc.at[zp, yl, pl.ds(0, 2)], dev(dy=1)),
-            (C0, mc.at[zp, yr, pl.ds(2, 2)], dev(dy=-1)),
+            (B0, line_b(zp, ul, 0), dev(du=1)),
+            (B1, line_b(zp, ur, 1), dev(du=-1)),
+            (C0, mc.at[slab_of(zp), vl, pl.ds(0, 2)], dev(dv=1)),
+            (C0, mc.at[slab_of(zp), vr, pl.ds(2, 2)], dev(dv=-1)),
         ]
         for n, (size, src, target) in enumerate(todo):
             arrive(zp, r_xy.at[5 * slot + n], size)
-            push(zp, src, target, s_xy.at[slot], r_xy.at[5 * slot + 4])
+            push(zp, src, target, s_xy, r_xy.at[5 * slot + 4])
 
     def at(d):
         return (z + d + NZ) % NZ
@@ -265,30 +290,47 @@
         ref, lane = (ma, 0) if j == 0 else (mb, min(j - 1, 3)) if j <= 3 or j == 7 else (mc, j - 4)
         return ref[zp, 2 * h:2 * h + 2, :, :, 128 * lane:128 * lane + 128].reshape(128, 128)
 
-    def compute(i):
-        zp = i
-
-        @pl.when(i < NZ - 1)
+    def own_rows(i):
+        return pfull[:, pl.ds(pl.multiple_of(MXU * i, MXU), MXU)]
+
+    def set_diagonal(i):
+        upper = blk(i, 0, 1)
+        wn[0:128, 0:128] = blk(i, 0, 0)
+        wn[0:128, 128:256] = upper
+        wn[128:256, 0:128] = upper.astype(F32).T.astype(BF16)
+        wn[128:256, 128:256] = blk(i, 1, 0)
+
+    def compute(zp, whole):
+        i = slab_of(zp)
+
+        @pl.when(zp != EMPTY)
         def _():
-            upper = blk(zp, 0, 1)
-            wn[0:128, 0:128] = blk(zp, 0, 0)
-            wn[0:128, 128:256] = upper
-            wn[128:256, 0:128] = upper.astype(F32).T.astype(BF16)
-            wn[128:256, 128:256] = blk(zp, 1, 0)
+            if whole:
+                set_diagonal(i)
             for d in (1, 2, 3):
-                wn[0:128, 256 * d:256 * d + 128] = blk(zp, 0, 2 * d)
-                wn[0:128, 256 * d + 128:256 * d + 256] = blk(zp, 0, 2 * d + 1)
-                wn[128:256, 256 * d:256 * d + 128] = blk(zp, 1, 2 * d - 1)
-                wn[128:256, 256 * d + 128:256 * d + 256] = blk(zp, 1, 2 * d)
-
-            own = pfull[:, pl.ds(pl.multiple_of(MXU * i, MXU), MXU)]
+                wn[0:128, 256 * d:256 * d + 128] = blk(i, 0, 2 * d)
+                wn[0:128, 256 * d + 128:256 * d + 256] = blk(i, 0, 2 * d + 1)
+                wn[128:256, 256 * d:256 * d + 128] = blk(i, 1, 2 * d - 1)
+                wn[128:256, 256 * d + 128:256 * d + 256] = blk(i, 1, 2 * d)
+            own = own_rows(i)
             for d in (1, 2, 3):
                 acc[(i + d) % 7] += nn(own, wn[:, 256 * d:256 * d + 256])
-            total = nn(own, wn[:, 0:256])
-            for d in (1, 2, 3):
-                cols = pl.ds(pl.multiple_of(MXU * ((i + d) % 7), MXU), MXU)
-                total += nt(pfull[:, cols], wn[:, 256 * d:256 * d + 256])
+            total = nt(own_rows((i + 1) % 7), wn[:, 256:512])
+            for d in (2, 3):
+                total += nt(own_rows((i + d) % 7), wn[:, 256 * d:256 * d + 256])
+            if whole:
+                total += nn(own, wn[:, 0:256])
             acc[i] += total
+
+    def diagonals():
+        @pl.loop(0, 3)
+        def _(n):
+            i = slab_of(at(n - 1))
+
+            @pl.when(at(n - 1) != EMPTY)
+            def _():
+                set_diagonal(i)
+                acc[i] += nn(own_rows(i), wn[:, 0:256])
 
     def forward(dist):
         for delta in ((0,) if dist == 0 else (4,) if dist == 4 else (-dist, dist)):
@@ -298,19 +340,15 @@
         for delta in ((0,) if dist == 0 else (4,) if dist == 4 else (-dist, dist)):
             arrive(at(delta), r_xy.at[5 * SLOT[delta] + 4], 2 * (B0 + B1) + C0)
         if dist in (0, 4):
-            compute(at(dist))
+            compute(at(dist), dist > 1)
         else:
             @pl.loop(0, 2)
             def _(n):
-                compute(at((2 * n - 1) * dist))
+                compute(at((2 * n - 1) * dist), dist > 1)
 
     arrive(z, r_1.at[0], 3 * TILE * 512)
-    for g in (0, 1):
-        z_send(g, 1, z, "b")
     xy_send(0, z, "b")
     arrive(z, r_1.at[1], 3 * TILE * 384)
-    for g in (0, 1):
-        z_send(g, 1, z, "c")
     xy_send(0, z, "c")
 
     A0 = 7 * TILE * 128
@@ -319,41 +357,42 @@
         pltpu.make_async_remote_copy(src, src, s_a.at[n], r_a.at[m], device_id=target,
                                      device_id_type=MESH).start()
 
-    @pl.when(z == NZ - 1)
+    @pl.when(z == EMPTY)
     def _():
         drain(r_a.at[0], A0)
 
-    @pl.when(z != NZ - 1)
+    @pl.when(z != EMPTY)
     def _():
         drain(r_a.at[0], 6 * TILE * 128)
 
     for d in (1, 2, 3):
-        push_a(ma.at[pl.ds(0, 7), y, x], dev(dx=d), 0, 1)
+        push_a(ma.at[:, v, u], dev(du=d), 0, 1)
     z_step(1, "b")
-    drain(r_a.at[1], 3 * A0)
-    push_a(ma.at[pl.ds(0, 7), y], dev(dy=1), 1, 2)
-    push_a(ma.at[pl.ds(0, 7), y], dev(dy=-1), 1, 3)
     z_step(1, "c")
     forward(0)
     z_step(2, "b")
     z_step(2, "c")
-    drain(r_a.at[2], 4 * A0)
-    push_a(ma.at[pl.ds(0, 7), (y + 3) % NY, pl.ds(0, 2)], dev(dy=1), 1, 4)
-    drain(r_a.at[3], 4 * A0)
-    push_a(ma.at[pl.ds(0, 7), (y + 1) % NY, pl.ds(2, 2)], dev(dy=-1), 1, 4)
+    drain(r_a.at[1], 3 * A0)
+    push_a(ma.at[:, v], dev(dv=1), 1, 2)
+    push_a(ma.at[:, v], dev(dv=-1), 1, 3)
     forward(1)
     z_step(3, "b")
     z_step(3, "c")
     z_step(4, "b")
     z_step(4, "c")
-    drain(r_a.at[4], 4 * A0)
     l_pd.wait()
     d_p.wait_recv()
     finish(0)
     forward(2)
+    drain(r_a.at[2], 4 * A0)
+    push_a(ma.at[:, (v + 3) % NY, pl.ds(0, 2)], dev(dv=1), 1, 4)
+    drain(r_a.at[3], 4 * A0)
+    push_a(ma.at[:, (v + 1) % NY, pl.ds(2, 2)], dev(dv=-1), 1, 4)
     finish(1)
     forward(3)
     forward(4)
+    drain(r_a.at[4], 4 * A0)
+    diagonals()
     finish(2)
     finish(3)
     finish(4)
@@ -380,6 +419,7 @@
     d_q.wait_send()
     drain(s_a.at[0], 3 * A0)
     drain(s_a.at[1], 12 * A0)
+    drain(s_xy, SLABS * 3 * (B0 + B1 + C0))
     for zp, sem, elements in sends:
         arrive(zp, sem, elements)
     for cond, copy in p0:
@@ -414,9 +454,9 @@
             pltpu.VMEM((ROWS, NG), BF16),
             pltpu.VMEM((2 * ROWS, HALF), BF16),
             pltpu.VMEM((ROWS, HALF), BF16),
-            pltpu.VMEM((NZ, NY, NX, TILE, 128), BF16),
-            pltpu.VMEM((NZ, NY, NX, TILE, 512), BF16),
-            pltpu.VMEM((NZ, NY, NX, TILE, 384), BF16),
+            pltpu.VMEM((SLABS, NY, NX, TILE, 128), BF16),
+            pltpu.VMEM((SLABS, NY, NX, TILE, 512), BF16),
+            pltpu.VMEM((SLABS, NY, NX, TILE, 384), BF16),
             pltpu.VMEM((7, ROWS, MXU), F32),
             pltpu.VMEM((2, TILE, WIN * BLK), BF16),
             pltpu.VMEM((OWN_ROWS, 2, HALF), BF16),
@@ -431,7 +471,7 @@
             dma(()), dma((2,)),
             dma((2,)), dma((5,)),
             dma((8,)), dma((16,)),
-            dma((8,)), dma((40,)),
+            dma(()), dma((40,)),
         ],
         compiler_params=pltpu.CompilerParams(
             collective_id=0, has_side_effects=True, vmem_limit_bytes=60 * 2**20),

time: 54.6 us -> 50.1 us (0.918)
  Pallas kernels: 52.4 us -> 47.8 us
    pallas_call x1, Pallas kernels: 52.4 us -> 47.8 us  [local(): pl.pallas_call(kernel, out_shape=jax.ShapeDtypeStruct((2, KP, SLOTS * PC)...]
where the time goes in v3:
time: 50.1 us; the launch traced here: 49.9 us
  Pallas kernels  47.8 us (95%)
  local copies, waits for them, and re-layouts  2.09 us (4%)
    pallas_call x1, Pallas kernels, local(): pl.pallas_call(kernel, out_shape=jax.ShapeDtypeStruct((2, KP, SLOTS * PC)...  47.8 us
    transpose x1, local copies, waits for them, and re-layouts, local(): return jnp.transpose(res, (1, 0, 2))  2.09 us

profile of v3, /device:TPU:1, one launch (start us, length us, event | category | flops | bytes accessed | tf_op | source)
XLA Modules:
  0.0 49.9 jit_solution(9440567659227122754)
XLA Ops:
  0.0 47.8 %shard_map.55 = f32[2,32,1600]{2,1,0:T(8,128)} custom-call(bf16[1280,896]{1,0:T(8,128)(2,1)} %bitcast.7, bf16[2560,896]{1,0:T(8,128)(2,1)} %bitcast.6, bf16[14,2,896]{2,1,0:T(2,128)(2,1)} %bitcast.8, s32[32]{0:T(128)} %cnt_in.1, s32[2,32]{1,0:T(2,128)} %bitcast.9), custom_call_target="tpu_custom_call" | custom-call | flops 8220835840 | bytes 8388608 | tf_op jit(solution)/shard_map/pallas_call | solution.py:445
  47.8 2.1 %copy.6 = f32[32,2,1600]{2,1,0:T(2,128)} copy(f32[32,2,1600]{2,0,1:T(8,128)} %bitcast.5) | data formatting | bytes 819200 | tf_op jit(solution)/shard_map/transpose | solution.py:486

commit v4 on v3

--- a/solution.py
+++ b/solution.py
@@ -370,11 +370,11 @@
     z_step(1, "b")
     z_step(1, "c")
     forward(0)
-    z_step(2, "b")
-    z_step(2, "c")
     drain(r_a.at[1], 3 * A0)
     push_a(ma.at[:, v], dev(dv=1), 1, 2)
     push_a(ma.at[:, v], dev(dv=-1), 1, 3)
+    z_step(2, "b")
+    z_step(2, "c")
     forward(1)
     z_step(3, "b")
     z_step(3, "c")

time: 50.1 us -> 49.7 us (level)
  no operation moved by 1% of the time
where the time goes in v4:
time: 49.7 us; the launch traced here: 49.6 us
  Pallas kernels  47.5 us (96%)
  local copies, waits for them, and re-layouts  2.09 us (4%)
    pallas_call x1, Pallas kernels, local(): pl.pallas_call(kernel, out_shape=jax.ShapeDtypeStruct((2, KP, SLOTS * PC)...  47.5 us
    transpose x1, local copies, waits for them, and re-layouts, local(): return jnp.transpose(res, (1, 0, 2))  2.09 us

profile of v4, /device:TPU:1, one launch (start us, length us, event | category | flops | bytes accessed | tf_op | source)
XLA Modules:
  0.0 49.6 jit_solution(92992207045706038)
XLA Ops:
  0.0 47.5 %shard_map.55 = f32[2,32,1600]{2,1,0:T(8,128)} custom-call(bf16[1280,896]{1,0:T(8,128)(2,1)} %bitcast.7, bf16[2560,896]{1,0:T(8,128)(2,1)} %bitcast.6, bf16[14,2,896]{2,1,0:T(2,128)(2,1)} %bitcast.8, s32[32]{0:T(128)} %cnt_in.1, s32[2,32]{1,0:T(2,128)} %bitcast.9), custom_call_target="tpu_custom_call" | custom-call | flops 8220835840 | bytes 8388608 | tf_op jit(solution)/shard_map/pallas_call | solution.py:445
  47.5 2.1 %copy.6 = f32[32,2,1600]{2,1,0:T(2,128)} copy(f32[32,2,1600]{2,0,1:T(8,128)} %bitcast.5) | data formatting | bytes 819200 | tf_op jit(solution)/shard_map/transpose | solution.py:486
